TPU v7x, 512 devices: a whole 4x8x8 slice. The times are simulated.
512 devices in a mesh: slab: 128 (over y, z, core), grp: 4 (over x).
Axes of the slice: x: 4, y: 8, z: 8, core: 2. Of those that a mesh axis runs over, the one named last changes fastest.
Arguments:
- a_blocks: bfloat16 [28672, 8, 64, 64], P(('slab', 'grp')), may hold values from -0.25 to 0.25
- neighbors: int32 [28672, 8], P(('slab', 'grp')), may hold values from 0 to 167, as said below
- prolong: bfloat16 [28672, 64, 64], P(('slab', 'grp')), may hold values from -2 to 2
- agg_ids: int32 [28672], P(('slab', 'grp')), may hold values from 0 to 7167, as said below
- coarse_prolong: bfloat16 [7168, 64, 64], P(('slab', 'grp')), may hold values from -0.75 to 0.75
- pairing: int32 [512, 7], P(('slab', 'grp')), may hold values from 0 to 13, as said below
Outputs:
- coarse_one: float32 [7168, 64, 64], P(('slab', 'grp'))
- coarse_two: float32 [3584, 64, 64], P(('slab', 'grp'))
Inputs may be any that keep to these rules, and one draw needn't show every extreme that they name: neighbors[r, 0] is the row itself, 56 + r % 56. The aggregate of a row is owned by a device of the same grp index: agg_ids[r] // 14 % 4 equals the grp index of the row's shard; its owner slab index agg_ids[r] // (14 * 4) lies in the five slabs from min(max(s - 2, 0), 128 - 5) on, where s is the slab index of the row's shard; the rows of one shard name at most 12 rows for one owner slab index, and that number is reached on every shard. `pairing`: rows s * 4 + 2h and s * 4 + 2h + 1 together hold each of 0 to 13 once.
All inputs are finite; a program needn't handle non-finite values.
Results may differ from a plain program's by a relative error of at most 0.0029.
Values may be sent and summed in bfloat16 or wider, within the bound.
A program may use at most 64 MiB of HBM per device.

v0:
```python
import jax
import jax.numpy as jnp
from jax import lax
from jax.sharding import PartitionSpec as P


def with_halo(cells, sides, width):
    for axis, dim in sides:
        count = lax.axis_size(axis)
        ends = count - 1
        head = lax.slice_in_dim(cells, 0, width, axis=dim)
        tail = lax.slice_in_dim(cells, cells.shape[dim] - width, cells.shape[dim], axis=dim)
        cells = jnp.concatenate(
            [
                lax.ppermute(tail, axis, [(i, (i + 1) % count) for i in range(ends)]),
                cells,
                lax.ppermute(head, axis, [((i + 1) % count, i) for i in range(ends)]),
            ],
            axis=dim,
        )
    return cells


def shifted(value, axis, steps):
    count = lax.axis_size(axis)
    leading, last = (max(0, -steps), min(count, count - steps))
    return lax.ppermute(value, axis, [(source, source + steps) for source in range(leading, last)])


def partner(value, axis, stride):
    mask = 2**stride
    pairs = [(source, source ^ mask) for source in range(lax.axis_size(axis))]
    return lax.ppermute(value, axis, pairs)


def galerkin(blocks, maps):
    inner = jnp.einsum("kbc,kcd->kbd", blocks, maps, precision=lax.Precision.HIGHEST)
    return jnp.einsum("kba,kbd->kad", maps, inner, precision=lax.Precision.HIGHEST)


def on_device(a_blocks, neighbors, prolong, agg_ids, coarse_prolong, pairing):
    rows = a_blocks.shape[0]
    width = a_blocks.shape[-1]
    agg_count = coarse_prolong.shape[0]
    groups = lax.axis_size("grp")
    capacity = (rows + 4) // 5
    buckets = 9
    extended = with_halo(prolong, (("slab", 0),), rows)
    picked = extended[neighbors]
    partial_w = jnp.einsum(
        "rnab,rnbc->rac", a_blocks, picked, preferred_element_type=jnp.float32
    ).astype(jnp.bfloat16)
    slab_here = lax.axis_index("slab")
    owner = agg_ids // (groups * agg_count)
    bucket = owner - slab_here + 4
    inside = agg_ids % agg_count
    order = jnp.arange(rows)
    same_bucket = bucket[:, None] == bucket[None, :]
    rank = jnp.sum(same_bucket & (order[None, :] < order[:, None]), axis=1)
    target = bucket * capacity + rank
    placed = target[None, :] == jnp.arange(buckets * capacity)[:, None]
    filled = jnp.any(placed, axis=1)
    slot_index = jnp.where(
        filled, jnp.sum(jnp.where(placed, inside[None, :], 0), axis=1), agg_count
    )
    slot_index = slot_index.reshape(buckets, capacity)
    parts = jnp.einsum(
        "rba,rbc->rac", prolong, partial_w, preferred_element_type=jnp.float32
    ).reshape(rows, -1)
    buffer = jnp.dot(placed.astype(jnp.float32), parts, precision=lax.Precision.HIGHEST)
    buffer = buffer.reshape(buckets, capacity, width * width)
    got_blocks = []
    got_indices = []
    for offset in range(-4, 5):
        piece = (buffer[offset + 4], slot_index[offset + 4])
        if offset != 0:
            piece = shifted((piece[0], piece[1]), "slab", offset)
        got_blocks.append(piece[0])
        got_indices.append(piece[1])
    arrived = jnp.concatenate(got_blocks, 0)
    got_index = jnp.concatenate(got_indices, 0)
    select = (got_index[None, :] == jnp.arange(agg_count)[:, None]).astype(jnp.float32)
    coarse_one = jnp.dot(select, arrived, precision=lax.Precision.HIGHEST).reshape(
        agg_count, width, width
    )
    half = agg_count // 2
    parity = lax.axis_index("grp") % 2
    local_k = parity * half + jnp.arange(half, dtype=jnp.int32)
    pair_row = pairing.reshape(-1)
    own_index = jnp.where(parity == 0, local_k, pair_row)
    partner_index = jnp.where(parity == 0, pair_row, local_k)
    maps = coarse_prolong.astype(jnp.float32)
    own_term = galerkin(coarse_one[own_index], maps[own_index])
    far_blocks, far_maps = partner((coarse_one, maps), "grp", 0)
    far_term = galerkin(far_blocks[partner_index], far_maps[partner_index])
    return (coarse_one, own_term + far_term)


def solution(mesh):
    placed = (
        P(("slab", "grp"), None, None, None),
        P(("slab", "grp"), None),
        P(("slab", "grp"), None, None),
        P(("slab", "grp")),
        P(("slab", "grp"), None, None),
        P(("slab", "grp"), None),
    )
    return jax.shard_map(
        on_device,
        mesh=mesh,
        in_specs=placed,
        out_specs=(P(("slab", "grp"), None, None), P(("slab", "grp"), None, None)),
        check_vma=False,
    )
```

profile of v0, /device:TPU:98, one launch (start us, length us, event | category | flops | bytes accessed | tf_op | source)
XLA Modules:
  0.0 194.8 jit_solution(7420668988308914323)
XLA Ops:
  2.6 2.4 %collective-permute-start.8 = (bf16[56,64,64]{2,1,0:T(8,128)(2,1)}, bf16[56,64,64]{2,1,0:T(8,128)(2,1)}, u32[]{:S(2)}, u32[]{:S(2)}) collective-permute-start(bf16[56,64,64]{2,1,0:T(8,128)(2,1)} %param.8), channel_id=1, source_target_pairs={{0,4},{4,8},{8,12},{12,16},{16,20},{20,24},{24,28},{28,32},{32,36}... | collective-permute-start | bytes 1376264 | tf_op jit(solution)/shard_map/ppermute | solution.py:15
  6.1 9.9 %collective-permute-start = (s32[12]{0:T(128)S(1)}, s32[12]{0:T(128)S(1)}, u32[]{:S(2)}, u32[]{:S(2)}) collective-permute-start(s32[12]{0:T(128)S(1)} %get-tuple-element.21), channel_id=1, source_target_pairs={{16,0},{20,4},{24,8},{28,12},{32,16},{36,20},{40,24},{44,28},{48,3... | collective-permute-start | bytes 152 | tf_op jit(solution)/shard_map/ppermute | solution.py:27
  17.0 2.4 %collective-permute-start.18 = (f32[14,64,64]{2,1,0:T(8,128)S(1)}, f32[14,64,64]{2,1,0:T(8,128)}, u32[]{:S(2)}, u32[]{:S(2)}) collective-permute-start(f32[14,64,64]{2,1,0:T(8,128)S(1)} %convert_element_type.14), channel_id=1, source_target_pairs={{0,1},{1,0},{2,3},{3,2},{4,5},{5,4},{6,7},{7,6},{8,9},{9,8},{10,11... | collective-permute-start | bytes 688136 | tf_op jit(solution)/shard_map/ppermute | solution.py:33
  21.4 2.3 %pad_maximum_fusion = bf16[168,64,64]{2,1,0:T(8,128)(2,1)S(1)} fusion(bf16[56,64,64]{2,1,0:T(8,128)(2,1)} %copy-done.1, bf16[56,64,64]{2,1,0:T(8,128)(2,1)} %param.8, bf16[56,64,64]{2,1,0:T(8,128)(2,1)} %collective-permute-done.8), kind=kLoop, calls=%fused_computation.5 | loop fusion | flops 1376256 | bytes 2752512 | tf_op jit(solution)/shard_map/concatenate | solution.py:13
  23.7 13.3 %gather_fusion = bf16[448,64,64]{2,1,0:T(8,128)(2,1)} fusion(bf16[168,64,64]{2,1,0:T(8,128)(2,1)S(1)} %pad_maximum_fusion, s32[1024]{0:T(1024)S(1)} %pad_clamp_fusion.2), kind=kCustom, calls=%fused_computation | custom fusion | bytes 7341824 | tf_op jit(solution)/shard_map/gather | solution.py:49
  37.1 7.7 %convolution_bitcast_fusion = f32[56,64,64]{1,2,0:T(8,128)S(1)} fusion(bf16[56,64,64]{2,1,0:T(8,128)(2,1)} %param.8, bf16[56,8,64,64]{3,2,1,0:T(8,128)(2,1)} %bitcast.32, bf16[56,8,64,64]{3,2,1,0:T(8,128)(2,1)} %param.6), kind=kOutput, calls=%fused_computation.7 | convolution fusion | flops 264470528 | bytes 8716288 | tf_op jit(solution)/shard_map/rba,rbc->rac/dot_general | solution.py:67
  49.8 6.1 %collective-permute-start.10 = (f32[12,4096]{1,0:T(8,128)S(1)}, f32[12,4096]{1,0:T(8,128)S(1)}, u32[]{:S(2)}, u32[]{:S(2)}) collective-permute-start(f32[12,4096]{1,0:T(8,128)S(1)} %get-tuple-element.10), channel_id=1, source_target_pairs={{16,0},{20,4},{24,8},{28,12},{32,16},{36,20},{40,24},{44,28},{48,3... | collective-permute-start | bytes 589832 | tf_op jit(solution)/shard_map/ppermute | solution.py:27
  56.0 3.9 %collective-permute-start.11 = (f32[12,4096]{1,0:T(8,128)S(1)}, f32[12,4096]{1,0:T(8,128)S(1)}, u32[]{:S(2)}, u32[]{:S(2)}) collective-permute-start(f32[12,4096]{1,0:T(8,128)S(1)} %get-tuple-element.9), channel_id=1, source_target_pairs={{12,0},{16,4},{20,8},{24,12},{28,16},{32,20},{36,24},{40,28},{44,3... | collective-permute-start | bytes 589832 | tf_op jit(solution)/shard_map/ppermute | solution.py:27
  59.9 3.2 %collective-permute-start.12 = (f32[12,4096]{1,0:T(8,128)S(1)}, f32[12,4096]{1,0:T(8,128)S(1)}, u32[]{:S(2)}, u32[]{:S(2)}) collective-permute-start(f32[12,4096]{1,0:T(8,128)S(1)} %get-tuple-element.8), channel_id=1, source_target_pairs={{8,0},{12,4},{16,8},{20,12},{24,16},{28,20},{32,24},{36,28},{40,32... | collective-permute-start | bytes 589832 | tf_op jit(solution)/shard_map/ppermute | solution.py:27
  65.1 14.4 %collective-permute-done.1 = s32[12]{0:T(128)S(1)} collective-permute-done((s32[12]{0:T(128)S(1)}, s32[12]{0:T(128)S(1)}, u32[]{:S(2)}, u32[]{:S(2)}) %collective-permute-start.1) | collective-permute-done | bytes 80 | tf_op jit(solution)/shard_map/ppermute | solution.py:27
  79.4 6.5 %collective-permute-start.2 = (s32[12]{0:T(128)S(1)}, s32[12]{0:T(128)S(1)}, u32[]{:S(2)}, u32[]{:S(2)}) collective-permute-start(s32[12]{0:T(128)S(1)} %get-tuple-element.19), channel_id=1, source_target_pairs={{8,0},{12,4},{16,8},{20,12},{24,16},{28,20},{32,24},{36,28},{40,32... | collective-permute-start | bytes 152 | tf_op jit(solution)/shard_map/ppermute | solution.py:27
  87.2 2.4 %collective-permute-start.3 = (s32[12]{0:T(128)S(1)}, s32[12]{0:T(128)S(1)}, u32[]{:S(2)}, u32[]{:S(2)}) collective-permute-start(s32[12]{0:T(128)S(1)} %get-tuple-element.18), channel_id=1, source_target_pairs={{4,0},{8,4},{12,8},{16,12},{20,16},{24,20},{28,24},{32,28},{36,32}... | collective-permute-start | bytes 152 | tf_op jit(solution)/shard_map/ppermute | solution.py:27
  92.9 2.8 %collective-permute-done.4 = s32[12]{0:T(128)S(1)} collective-permute-done((s32[12]{0:T(128)S(1)}, s32[12]{0:T(128)S(1)}, u32[]{:S(2)}, u32[]{:S(2)}) %collective-permute-start.4) | collective-permute-done | bytes 80 | tf_op jit(solution)/shard_map/ppermute | solution.py:27
  97.7 8.4 %collective-permute-done.5 = s32[12]{0:T(128)S(1)} collective-permute-done((s32[12]{0:T(128)S(1)}, s32[12]{0:T(128)S(1)}, u32[]{:S(2)}, u32[]{:S(2)}) %collective-permute-start.5) | collective-permute-done | bytes 80 | tf_op jit(solution)/shard_map/ppermute | solution.py:27
  108.0 7.2 %collective-permute-done.6 = s32[12]{0:T(128)S(1)} collective-permute-done((s32[12]{0:T(128)S(1)}, s32[12]{0:T(128)S(1)}, u32[]{:S(2)}, u32[]{:S(2)}) %collective-permute-start.6) | collective-permute-done | bytes 80 | tf_op jit(solution)/shard_map/ppermute | solution.py:27
  117.0 7.7 %collective-permute-done.7 = s32[12]{0:T(128)S(1)} collective-permute-done((s32[12]{0:T(128)S(1)}, s32[12]{0:T(128)S(1)}, u32[]{:S(2)}, u32[]{:S(2)}) %collective-permute-start.7) | collective-permute-done | bytes 80 | tf_op jit(solution)/shard_map/ppermute | solution.py:27
  126.7 2.4 %collective-permute-start.14 = (f32[12,4096]{1,0:T(8,128)S(1)}, f32[12,4096]{1,0:T(8,128)S(1)}, u32[]{:S(2)}, u32[]{:S(2)}) collective-permute-start(f32[12,4096]{1,0:T(8,128)S(1)} %get-tuple-element.5), channel_id=1, source_target_pairs={{0,4},{4,8},{8,12},{12,16},{16,20},{20,24},{24,28},{28,32},{32,36}... | collective-permute-start | bytes 589832 | tf_op jit(solution)/shard_map/ppermute | solution.py:27
  129.1 2.5 %collective-permute-start.15 = (f32[12,4096]{1,0:T(8,128)S(1)}, f32[12,4096]{1,0:T(8,128)}, u32[]{:S(2)}, u32[]{:S(2)}) collective-permute-start(f32[12,4096]{1,0:T(8,128)S(1)} %get-tuple-element.4), channel_id=1, source_target_pairs={{0,8},{4,12},{8,16},{12,20},{16,24},{20,28},{24,32},{28,36},{32,40... | collective-permute-start | bytes 589832 | tf_op jit(solution)/shard_map/ppermute | solution.py:27
  133.6 2.1 %collective-permute-start.17 = (f32[12,4096]{1,0:T(8,128)S(1)}, f32[12,4096]{1,0:T(8,128)}, u32[]{:S(2)}, u32[]{:S(2)}) collective-permute-start(f32[12,4096]{1,0:T(8,128)S(1)} %get-tuple-element.2), channel_id=1, source_target_pairs={{0,16},{4,20},{8,24},{12,28},{16,32},{20,36},{24,40},{28,44},{32,4... | collective-permute-start | bytes 589832 | tf_op jit(solution)/shard_map/ppermute | solution.py:27
  138.2 5.5 %collective-permute-done.15 = f32[12,4096]{1,0:T(8,128)} collective-permute-done((f32[12,4096]{1,0:T(8,128)S(1)}, f32[12,4096]{1,0:T(8,128)}, u32[]{:S(2)}, u32[]{:S(2)}) %collective-permute-start.15) | collective-permute-done | bytes 196640 | tf_op jit(solution)/shard_map/ppermute | solution.py:27
  143.7 17.9 %collective-permute-done.16 = f32[12,4096]{1,0:T(8,128)} collective-permute-done((f32[12,4096]{1,0:T(8,128)S(1)}, f32[12,4096]{1,0:T(8,128)}, u32[]{:S(2)}, u32[]{:S(2)}) %collective-permute-start.16) | collective-permute-done | bytes 196640 | tf_op jit(solution)/shard_map/ppermute | solution.py:27
  161.6 6.3 %collective-permute-done.17 = f32[12,4096]{1,0:T(8,128)} collective-permute-done((f32[12,4096]{1,0:T(8,128)S(1)}, f32[12,4096]{1,0:T(8,128)}, u32[]{:S(2)}, u32[]{:S(2)}) %collective-permute-start.17) | collective-permute-done | bytes 196640 | tf_op jit(solution)/shard_map/ppermute | solution.py:27
  167.9 9.1 %concatenate.11 = f32[108,4096]{1,0:T(8,128)S(1)} concatenate(f32[12,4096]{1,0:T(8,128)S(1)} %collective-permute-done.10, f32[12,4096]{1,0:T(8,128)} %copy-done.3, f32[12,4096]{1,0:T(8,128)} %copy-done.4, f32[12,4096]{1,0:T(8,128)} %collective-permute-done.13, f32[12,4096]{1,0:T(8,128)S(1)} %get-tuple-element.6, f32[12,4096]{1,0:T(8,128)S(1)} %collective-permute-done.14, ...), dimensions={0} | concatenate | bytes 3538944 | tf_op jit(solution)/shard_map/concatenate | solution.py:80
  181.1 11.5 %collective-permute-done.19 = f32[14,64,64]{2,1,0:T(8,128)S(1)} collective-permute-done((f32[14,64,64]{2,1,0:T(8,128)S(1)}, f32[14,64,64]{2,1,0:T(8,128)S(1)}, u32[]{:S(2)}, u32[]{:S(2)}) %collective-permute-start.19) | collective-permute-done | bytes 229408 | tf_op jit(solution)/shard_map/ppermute | solution.py:33
  (62 shorter events, 35.7 us)
Async XLA Ops:
  0.6 19.8 %collective-permute-start.9 = (bf16[56,64,64]{2,1,0:T(8,128)(2,1)}, bf16[56,64,64]{2,1,0:T(8,128)(2,1)S(1)}, u32[]{:S(2)}, u32[]{:S(2)}) collective-permute-start(bf16[56,64,64]{2,1,0:T(8,128)(2,1)} %param.8), channel_id=1, source_target_pairs={{4,0},{8,4},{12,8},{16,12},{20,16},{24,20},{28,24},{32,28},{36,32}... | collective-permute-start | bytes 1376264 | tf_op jit(solution)/shard_map/ppermute | solution.py:17
  2.6 18.8 %collective-permute-start.8 = (bf16[56,64,64]{2,1,0:T(8,128)(2,1)}, bf16[56,64,64]{2,1,0:T(8,128)(2,1)}, u32[]{:S(2)}, u32[]{:S(2)}) collective-permute-start(bf16[56,64,64]{2,1,0:T(8,128)(2,1)} %param.8), channel_id=1, source_target_pairs={{0,4},{4,8},{8,12},{12,16},{16,20},{20,24},{24,28},{28,32},{32,36}... | collective-permute-start | bytes 1376264 | tf_op jit(solution)/shard_map/ppermute | solution.py:15
  6.1 57.0 %collective-permute-start = (s32[12]{0:T(128)S(1)}, s32[12]{0:T(128)S(1)}, u32[]{:S(2)}, u32[]{:S(2)}) collective-permute-start(s32[12]{0:T(128)S(1)} %get-tuple-element.21), channel_id=1, source_target_pairs={{16,0},{20,4},{24,8},{28,12},{32,16},{36,20},{40,24},{44,28},{48,3... | collective-permute-start | bytes 152 | tf_op jit(solution)/shard_map/ppermute | solution.py:27
  17.0 109.6 %collective-permute-start.18 = (f32[14,64,64]{2,1,0:T(8,128)S(1)}, f32[14,64,64]{2,1,0:T(8,128)}, u32[]{:S(2)}, u32[]{:S(2)}) collective-permute-start(f32[14,64,64]{2,1,0:T(8,128)S(1)} %convert_element_type.14), channel_id=1, source_target_pairs={{0,1},{1,0},{2,3},{3,2},{4,5},{5,4},{6,7},{7,6},{8,9},{9,8},{10,11... | collective-permute-start | bytes 688136 | tf_op jit(solution)/shard_map/ppermute | solution.py:33
  49.6 86.1 %copy-start.2 = (bf16[14,64,64]{2,1,0:T(8,128)(2,1)S(1)}, bf16[14,64,64]{2,1,0:T(8,128)(2,1)}, u32[]{:S(2)}) copy-start(bf16[14,64,64]{2,1,0:T(8,128)(2,1)} %param.10) | copy-start | bytes 344068
  49.8 79.3 %collective-permute-start.10 = (f32[12,4096]{1,0:T(8,128)S(1)}, f32[12,4096]{1,0:T(8,128)S(1)}, u32[]{:S(2)}, u32[]{:S(2)}) collective-permute-start(f32[12,4096]{1,0:T(8,128)S(1)} %get-tuple-element.10), channel_id=1, source_target_pairs={{16,0},{20,4},{24,8},{28,12},{32,16},{36,20},{40,24},{44,28},{48,3... | collective-permute-start | bytes 589832 | tf_op jit(solution)/shard_map/ppermute | solution.py:27
  56.0 75.6 %collective-permute-start.11 = (f32[12,4096]{1,0:T(8,128)S(1)}, f32[12,4096]{1,0:T(8,128)S(1)}, u32[]{:S(2)}, u32[]{:S(2)}) collective-permute-start(f32[12,4096]{1,0:T(8,128)S(1)} %get-tuple-element.9), channel_id=1, source_target_pairs={{12,0},{16,4},{20,8},{24,12},{28,16},{32,20},{36,24},{40,28},{44,3... | collective-permute-start | bytes 589832 | tf_op jit(solution)/shard_map/ppermute | solution.py:27
  59.9 73.7 %collective-permute-start.12 = (f32[12,4096]{1,0:T(8,128)S(1)}, f32[12,4096]{1,0:T(8,128)S(1)}, u32[]{:S(2)}, u32[]{:S(2)}) collective-permute-start(f32[12,4096]{1,0:T(8,128)S(1)} %get-tuple-element.8), channel_id=1, source_target_pairs={{8,0},{12,4},{16,8},{20,12},{24,16},{28,20},{32,24},{36,28},{40,32... | collective-permute-start | bytes 589832 | tf_op jit(solution)/shard_map/ppermute | solution.py:27
  63.2 16.3 %collective-permute-start.1 = (s32[12]{0:T(128)S(1)}, s32[12]{0:T(128)S(1)}, u32[]{:S(2)}, u32[]{:S(2)}) collective-permute-start(s32[12]{0:T(128)S(1)} %get-tuple-element.20), channel_id=1, source_target_pairs={{12,0},{16,4},{20,8},{24,12},{28,16},{32,20},{36,24},{40,28},{44,3... | collective-permute-start | bytes 152 | tf_op jit(solution)/shard_map/ppermute | solution.py:27
  79.4 7.7 %collective-permute-start.2 = (s32[12]{0:T(128)S(1)}, s32[12]{0:T(128)S(1)}, u32[]{:S(2)}, u32[]{:S(2)}) collective-permute-start(s32[12]{0:T(128)S(1)} %get-tuple-element.19), channel_id=1, source_target_pairs={{8,0},{12,4},{16,8},{20,12},{24,16},{28,20},{32,24},{36,28},{40,32... | collective-permute-start | bytes 152 | tf_op jit(solution)/shard_map/ppermute | solution.py:27
  87.2 3.7 %collective-permute-start.3 = (s32[12]{0:T(128)S(1)}, s32[12]{0:T(128)S(1)}, u32[]{:S(2)}, u32[]{:S(2)}) collective-permute-start(s32[12]{0:T(128)S(1)} %get-tuple-element.18), channel_id=1, source_target_pairs={{4,0},{8,4},{12,8},{16,12},{20,16},{24,20},{28,24},{32,28},{36,32}... | collective-permute-start | bytes 152 | tf_op jit(solution)/shard_map/ppermute | solution.py:27
  90.9 4.8 %collective-permute-start.4 = (s32[12]{0:T(128)S(1)}, s32[12]{0:T(128)S(1)}, u32[]{:S(2)}, u32[]{:S(2)}) collective-permute-start(s32[12]{0:T(128)S(1)} %get-tuple-element.16), channel_id=1, source_target_pairs={{0,4},{4,8},{8,12},{12,16},{16,20},{20,24},{24,28},{28,32},{32,36}... | collective-permute-start | bytes 152 | tf_op jit(solution)/shard_map/ppermute | solution.py:27
  95.7 10.3 %collective-permute-start.5 = (s32[12]{0:T(128)S(1)}, s32[12]{0:T(128)S(1)}, u32[]{:S(2)}, u32[]{:S(2)}) collective-permute-start(s32[12]{0:T(128)S(1)} %get-tuple-element.15), channel_id=1, source_target_pairs={{0,8},{4,12},{8,16},{12,20},{16,24},{20,28},{24,32},{28,36},{32,40... | collective-permute-start | bytes 152 | tf_op jit(solution)/shard_map/ppermute | solution.py:27
  106.0 9.1 %collective-permute-start.6 = (s32[12]{0:T(128)S(1)}, s32[12]{0:T(128)S(1)}, u32[]{:S(2)}, u32[]{:S(2)}) collective-permute-start(s32[12]{0:T(128)S(1)} %get-tuple-element.14), channel_id=1, source_target_pairs={{0,12},{4,16},{8,20},{12,24},{16,28},{20,32},{24,36},{28,40},{32,4... | collective-permute-start | bytes 152 | tf_op jit(solution)/shard_map/ppermute | solution.py:27
  115.1 9.6 %collective-permute-start.7 = (s32[12]{0:T(128)S(1)}, s32[12]{0:T(128)S(1)}, u32[]{:S(2)}, u32[]{:S(2)}) collective-permute-start(s32[12]{0:T(128)S(1)} %get-tuple-element.13), channel_id=1, source_target_pairs={{0,16},{4,20},{8,24},{12,28},{16,32},{20,36},{24,40},{28,44},{32,4... | collective-permute-start | bytes 152 | tf_op jit(solution)/shard_map/ppermute | solution.py:27
  124.8 13.2 %collective-permute-start.13 = (f32[12,4096]{1,0:T(8,128)S(1)}, f32[12,4096]{1,0:T(8,128)}, u32[]{:S(2)}, u32[]{:S(2)}) collective-permute-start(f32[12,4096]{1,0:T(8,128)S(1)} %get-tuple-element.7), channel_id=1, source_target_pairs={{4,0},{8,4},{12,8},{16,12},{20,16},{24,20},{28,24},{32,28},{36,32}... | collective-permute-start | bytes 589832 | tf_op jit(solution)/shard_map/ppermute | solution.py:27
  126.7 11.5 %collective-permute-start.14 = (f32[12,4096]{1,0:T(8,128)S(1)}, f32[12,4096]{1,0:T(8,128)S(1)}, u32[]{:S(2)}, u32[]{:S(2)}) collective-permute-start(f32[12,4096]{1,0:T(8,128)S(1)} %get-tuple-element.5), channel_id=1, source_target_pairs={{0,4},{4,8},{8,12},{12,16},{16,20},{20,24},{24,28},{28,32},{32,36}... | collective-permute-start | bytes 589832 | tf_op jit(solution)/shard_map/ppermute | solution.py:27
  129.1 14.6 %collective-permute-start.15 = (f32[12,4096]{1,0:T(8,128)S(1)}, f32[12,4096]{1,0:T(8,128)}, u32[]{:S(2)}, u32[]{:S(2)}) collective-permute-start(f32[12,4096]{1,0:T(8,128)S(1)} %get-tuple-element.4), channel_id=1, source_target_pairs={{0,8},{4,12},{8,16},{12,20},{16,24},{20,28},{24,32},{28,36},{32,40... | collective-permute-start | bytes 589832 | tf_op jit(solution)/shard_map/ppermute | solution.py:27
  131.6 36.3 %copy-start.3 = (f32[12,4096]{1,0:T(8,128)}, f32[12,4096]{1,0:T(8,128)S(1)}, u32[]{:S(2)}) copy-start(f32[12,4096]{1,0:T(8,128)S(1)} %collective-permute-done.11) | copy-start | bytes 589828
  131.6 30.0 %collective-permute-start.16 = (f32[12,4096]{1,0:T(8,128)S(1)}, f32[12,4096]{1,0:T(8,128)}, u32[]{:S(2)}, u32[]{:S(2)}) collective-permute-start(f32[12,4096]{1,0:T(8,128)S(1)} %get-tuple-element.3), channel_id=1, source_target_pairs={{0,12},{4,16},{8,20},{12,24},{16,28},{20,32},{24,36},{28,40},{32,4... | collective-permute-start | bytes 589832 | tf_op jit(solution)/shard_map/ppermute | solution.py:27
  133.6 34.3 %copy-start.4 = (f32[12,4096]{1,0:T(8,128)}, f32[12,4096]{1,0:T(8,128)S(1)}, u32[]{:S(2)}) copy-start(f32[12,4096]{1,0:T(8,128)S(1)} %collective-permute-done.12) | copy-start | bytes 589828
  133.6 34.3 %collective-permute-start.17 = (f32[12,4096]{1,0:T(8,128)S(1)}, f32[12,4096]{1,0:T(8,128)}, u32[]{:S(2)}, u32[]{:S(2)}) collective-permute-start(f32[12,4096]{1,0:T(8,128)S(1)} %get-tuple-element.2), channel_id=1, source_target_pairs={{0,16},{4,20},{8,24},{12,28},{16,32},{20,36},{24,40},{28,44},{32,4... | collective-permute-start | bytes 589832 | tf_op jit(solution)/shard_map/ppermute | solution.py:27
  177.9 16.9 %copy-start = (f32[14,64,64]{2,1,0:T(8,128)}, f32[14,64,64]{2,1,0:T(8,128)S(1)}, u32[]{:S(2)}) copy-start(f32[14,64,64]{2,1,0:T(8,128)S(1)} %reshape.103) | copy-start | bytes 688132
  178.5 14.1 %collective-permute-start.19 = (f32[14,64,64]{2,1,0:T(8,128)S(1)}, f32[14,64,64]{2,1,0:T(8,128)S(1)}, u32[]{:S(2)}, u32[]{:S(2)}) collective-permute-start(f32[14,64,64]{2,1,0:T(8,128)S(1)} %reshape.103), channel_id=1, source_target_pairs={{0,1},{1,0},{2,3},{3,2},{4,5},{5,4},{6,7},{7,6},{8,9},{9,8},{10,11... | collective-permute-start | bytes 688136 | tf_op jit(solution)/shard_map/ppermute | solution.py:33
  (2 other events, 14.5 us)
where the time goes:
time: 196 us; the launch traced here: 195 us
  waiting for transfers between devices  84.4 us (43%)
  starting transfers between devices  61.4 us (31%)
  local copies, waits for them, and re-layouts  31.3 us (16%)
  matrix products  11.5 us (6%)
  other arithmetic  5.08 us (3%)
    ppermute x16, waiting for transfers between devices, shifted(): lax.ppermute(value, axis, [(source, source + steps) for source in range(l...  72.9 us
    ppermute x16, starting transfers between devices, shifted(): lax.ppermute(value, axis, [(source, source + steps) for source in range(l...  52.6 us
    gather x1, local copies, waits for them, and re-layouts, on_device(): picked = extended[neighbors]  13.3 us
    ppermute x2, waiting for transfers between devices, partner(): return lax.ppermute(value, axis, pairs)  11.5 us
    concatenate x1, local copies, waits for them, and re-layouts, on_device(): arrived = jnp.concatenate(got_blocks, 0)  9.14 us
    dot_general x1, matrix products, on_device(): jnp.einsum('rba,rbc->rac', prolong, partial_w, preferred_element_type=jnp...  7.71 us
    ppermute x2, starting transfers between devices, partner(): return lax.ppermute(value, axis, pairs)  4.47 us
  transfers between devices with their start and end apart: 20, of which 12 were waited for; matrix products, arithmetic and copies ran while one was open for 18% of the time, Pallas kernels for 0%

commit v1 on v0

v1 whole, which is shorter than its diff:
```python
import functools

import jax
import jax.numpy as jnp
from jax import lax
from jax.experimental import pallas as pl
from jax.experimental.pallas import tpu as pltpu
from jax.sharding import PartitionSpec as P

MESH = pl.DeviceIdType.MESH
WINDOW = 5
REACH = WINDOW - 1
CHUNKS = 4
F32 = jnp.float32
BF16 = jnp.bfloat16


def fold(block):
    half = block.shape[0] // 2
    return jnp.concatenate([block[:half], block[half:]], axis=1)


def unfold(block):
    width = block.shape[1] // 2
    return jnp.concatenate([block[:, :width], block[:, width:]], axis=0)


def galerkin(block, map_t, map_):
    high = block.astype(BF16)
    low = (block - high.astype(F32)).astype(BF16)
    inner = jnp.dot(map_t, high, preferred_element_type=F32) + jnp.dot(
        map_t, low, preferred_element_type=F32
    )
    high = inner.astype(BF16)
    low = (inner - high.astype(F32)).astype(BF16)
    return jnp.dot(high, map_, preferred_element_type=F32) + jnp.dot(
        low, map_, preferred_element_type=F32
    )


def kernel(
    sizes,
    nbr, agg, pair, a_hbm, p_hbm, m_hbm,
    one_hbm, two_hbm,
    a_buf, a_cat, ext, p_fold, halo, p_t, m_buf, m_t, run, send, recv, acc, one_buf, two_buf, tx, rx, tab_v, tab,
    a_sem, in_sem, tab_sem, out_sem, halo_send, halo_recv, part_send, part_recv, pair_send, pair_recv,
):
    n_slab, n_grp, rows, slots, width, aggs = sizes
    half = aggs // 2
    capacity = (rows + WINDOW - 1) // WINDOW
    slab = lax.axis_index("slab")
    grp = lax.axis_index("grp")

    def window(s):
        return jnp.clip(s - WINDOW // 2, 0, n_slab - WINDOW)

    first = window(slab)
    chip_mate = slab + 1 - 2 * (slab % 2)
    grp_mate = grp + 1 - 2 * (grp % 2)
    parity = grp % 2

    p_copy = pltpu.make_async_copy(p_hbm, ext.at[pl.ds(rows, rows)], in_sem.at[0])
    p_copy.start()
    m_copy = pltpu.make_async_copy(m_hbm, m_buf, in_sem.at[1])
    a_chunks = a_sem.shape[0]
    a_rows = rows // a_chunks
    a_copies = [
        pltpu.make_async_copy(a_hbm.at[pl.ds(i * a_rows, a_rows)], a_buf.at[pl.ds(i * a_rows, a_rows)], a_sem.at[i])
        for i in range(a_chunks)
    ]
    for copy in a_copies:
        copy.start()
    m_copy.start()

    barrier = pltpu.get_barrier_semaphore()

    def sends_here(offset):
        source = slab + offset
        low = window(source)
        return (source >= 0) & (source < n_slab) & (low <= slab) & (slab < low + WINDOW)

    for offset in range(-REACH, REACH + 1):
        if offset != 0:
            @pl.when(sends_here(offset))
            def _():
                pl.semaphore_signal(barrier, inc=1, device_id=(slab + offset, grp), device_id_type=MESH)
    pl.semaphore_signal(barrier, inc=1, device_id=(slab, grp_mate), device_id_type=MESH)

    p_copy.wait()
    per = rows // CHUNKS

    def halo_copy(side, chunk):
        span = pl.ds(chunk * per, per)
        target = slab + 1 - 2 * side
        return pltpu.make_async_remote_copy(
            src_ref=p_fold.at[span],
            dst_ref=halo.at[side, span],
            send_sem=halo_send.at[side, chunk],
            recv_sem=halo_recv.at[side, chunk],
            device_id=(target, grp),
            device_id_type=MESH,
        )

    has_next = slab < n_slab - 1
    has_previous = slab > 0
    for chunk in range(CHUNKS):
        def fold_row(r, _, chunk=chunk):
            p_fold[chunk * per + r] = fold(ext[rows + chunk * per + r])
            return 0

        lax.fori_loop(0, per, fold_row, 0, unroll=2)
        if chunk == 0:
            pl.semaphore_wait(barrier, WINDOW)

        @pl.when(has_next)
        def _():
            halo_copy(0, chunk).start()

        @pl.when(has_previous)
        def _():
            halo_copy(1, chunk).start()

    tag = []
    for j in range(WINDOW):
        owner = first + j
        kind = jnp.where(owner == slab, 2, jnp.where(owner == chip_mate, 1, 0))
        tag.append(kind * WINDOW + j)
    place = [sum((tag[i] < tag[j]).astype(jnp.int32) for i in range(WINDOW)) for j in range(WINDOW)]
    bucket_of = [
        sum(jnp.where(place[j] == q, j, 0) for j in range(WINDOW)) for q in range(WINDOW)
    ]
    tall = 64
    sub = lax.broadcasted_iota(jnp.int32, (tall, 128), 0)
    lane = lax.broadcasted_iota(jnp.int32, (tall, 128), 1)
    lane_row = lax.broadcasted_iota(jnp.int32, (1, 128), 1)
    tab_v[...] = jnp.zeros_like(tab_v)
    tab_v[0:1, 0:rows] = agg[...]
    ids = tab_v[0:1, :]
    owner_row = lax.div(ids, jnp.int32(n_grp * aggs))
    inside = lax.rem(ids, jnp.int32(aggs))
    bucket = owner_row - first
    at = jnp.zeros_like(bucket)
    for j in range(WINDOW):
        at = at + jnp.where(bucket == j, place[j], 0)
    far = 1000
    key_row = jnp.where(lane_row < rows, at * aggs + inside, far).astype(F32)
    keys = jnp.broadcast_to(key_row, (tall, 128))
    key_col = jnp.sum(jnp.where(sub == lane, keys, 0.0), axis=1, keepdims=True)
    less = (keys < key_col) | ((keys == key_col) & (lane < sub))
    rank = jnp.sum(jnp.where(less, 1.0, 0.0), axis=1, keepdims=True)
    lane_f = lane.astype(F32)
    hit = rank == lane_f
    order_row = jnp.sum(jnp.where(hit, sub.astype(F32), 0.0), axis=0, keepdims=True)
    sorted_row = jnp.sum(jnp.where(hit, key_col, 0.0), axis=0, keepdims=True)
    same = (sorted_row == pltpu.roll(sorted_row, 1, 1)) & (lane_row > 0)
    before_row = jnp.where(same, lane_row - 1, rows)
    upto = jnp.sum(jnp.where(key_col <= lane_f, 1.0, 0.0), axis=0, keepdims=True)
    below = jnp.sum(jnp.where(key_col < lane_f, 1.0, 0.0), axis=0, keepdims=True)
    last_row = jnp.where(upto > below, upto - 1.0, float(rows))
    named_row = jnp.zeros((tall, 128), F32)
    named_col = jnp.zeros((tall, 128), F32)
    for i in range(half):
        named_row = named_row + jnp.where(lane == pair[0, i], 1.0, 0.0)
        named_col = named_col + jnp.where(sub == pair[0, i], 1.0, 0.0)
    free_row = (named_row == 0.0) & (lane < aggs)
    free_col = (named_col == 0.0) & (sub < aggs)
    rank_free = jnp.sum(jnp.where(free_row & (lane < sub), 1.0, 0.0), axis=1, keepdims=True)
    rest_row = jnp.sum(
        jnp.where(free_col & (rank_free == lane_f), sub.astype(F32), 0.0), axis=0, keepdims=True
    )
    tab_v[0:1, :] = order_row.astype(jnp.int32)
    tab_v[1:2, :] = before_row
    tab_v[2:3, :] = last_row.astype(jnp.int32)
    tab_v[3:4, :] = rest_row.astype(jnp.int32)
    tab_copy = pltpu.make_async_copy(tab_v, tab, tab_sem)
    tab_copy.start()

    run[rows] = jnp.zeros((width, width), F32)
    for i in range(a_chunks):
        a_copies[i].wait()

        def lay(r, _, i=i):
            row = i * a_rows + r
            a_cat[row] = jnp.concatenate([a_buf[row, n] for n in range(slots)], axis=1)
            p_t[row] = ext[rows + row].T
            return 0

        lax.fori_loop(0, a_rows, lay, 0, unroll=2)
    m_copy.wait()

    def turn(k, _):
        m_t[k] = m_buf[k].T
        return 0

    lax.fori_loop(0, aggs, turn, 0, unroll=2)
    tab_copy.wait()

    for side, there in ((0, has_previous), (1, has_next)):
        base = side * 2 * rows

        @pl.when(jnp.logical_not(there))
        def _():
            def clear(r, _):
                ext[base + r] = jnp.zeros((width, width), BF16)
                return 0

            lax.fori_loop(0, rows, clear, 0, unroll=2)

    for chunk in range(CHUNKS):
        for side, there in ((0, has_previous), (1, has_next)):
            base = side * 2 * rows + chunk * per

            @pl.when(there)
            def _():
                halo_copy(side, chunk).wait_recv()

                def open_row(r, _):
                    ext[base + r] = unfold(halo[side, chunk * per + r])
                    return 0

                lax.fori_loop(0, per, open_row, 0, unroll=2)

    def part_copy(q):
        owner = first + bucket_of[q]
        at_owner = slab - owner + REACH
        return pltpu.make_async_remote_copy(
            src_ref=send.at[q],
            dst_ref=recv.at[at_owner],
            send_sem=part_send.at[q],
            recv_sem=part_recv.at[at_owner],
            device_id=(owner, grp),
            device_id_type=MESH,
        )

    def row_step(k, _):
        r = jnp.clip(tab[0, k], 0, rows - 1)
        picked = jnp.concatenate([ext[nbr[r, n]] for n in range(slots)], axis=0)
        partial_w = jnp.dot(a_cat[r], picked, preferred_element_type=F32).astype(BF16)
        part = jnp.dot(p_t[r], partial_w, preferred_element_type=F32)
        run[k] = part + run[jnp.clip(tab[1, k], 0, rows)]
        return 0

    for q in range(WINDOW):
        begin, end = q * capacity, min((q + 1) * capacity, rows)
        lax.fori_loop(begin, end, row_step, 0, unroll=4)

        def gather(k, _, q=q):
            block = fold(run[jnp.clip(tab[2, q * aggs + k], 0, rows)])
            if q < REACH:
                send[q, k] = block.astype(BF16)
            else:
                acc[k] = block
            return 0

        lax.fori_loop(0, aggs, gather, 0, unroll=2)
        if q < REACH:
            part_copy(q).start()

    offsets = sorted((d for d in range(-REACH, REACH + 1) if d != 0), key=abs)
    for offset in offsets:
        at_here = offset + REACH

        @pl.when(sends_here(offset))
        def _():
            pltpu.make_async_remote_copy(
                src_ref=recv.at[at_here],
                dst_ref=recv.at[at_here],
                send_sem=part_send.at[0],
                recv_sem=part_recv.at[at_here],
                device_id=(slab, grp),
                device_id_type=MESH,
            ).wait_recv()
            acc[...] += recv[at_here].astype(F32)

    def open_sum(k, _):
        one_buf[k] = unfold(acc[k])
        return 0

    lax.fori_loop(0, aggs, open_sum, 0, unroll=2)
    one_copy = pltpu.make_async_copy(one_buf, one_hbm, out_sem.at[0])
    one_copy.start()

    def away(t, _):
        k = jnp.where(parity == 0, half + t, jnp.clip(tab[3, t], 0, aggs - 1))
        tx[t] = fold(galerkin(one_buf[k], m_t[k], m_buf[k])).astype(BF16)
        return 0

    lax.fori_loop(0, half, away, 0, unroll=half)
    pair_copy = pltpu.make_async_remote_copy(
        src_ref=tx, dst_ref=rx, send_sem=pair_send, recv_sem=pair_recv,
        device_id=(slab, grp_mate), device_id_type=MESH,
    )
    pair_copy.start()

    def home(t, _):
        k = jnp.where(parity == 0, t, pair[0, t])
        two_buf[t] = galerkin(one_buf[k], m_t[k], m_buf[k])
        return 0

    lax.fori_loop(0, half, home, 0, unroll=half)
    pair_copy.wait_recv()
    for t in range(half):
        before = sum((pair[0, i] < pair[0, t]).astype(jnp.int32) for i in range(half))
        at_rx = jnp.where(parity == 0, before, t)
        two_buf[t] += unfold(rx[at_rx].astype(F32))
    two_copy = pltpu.make_async_copy(two_buf, two_hbm, out_sem.at[1])
    two_copy.start()

    pair_copy.wait_send()
    for q in range(REACH):
        part_copy(q).wait_send()
    for chunk in range(CHUNKS):
        @pl.when(has_next)
        def _():
            halo_copy(0, chunk).wait_send()

        @pl.when(has_previous)
        def _():
            halo_copy(1, chunk).wait_send()
    one_copy.wait()
    two_copy.wait()


def on_device(n_slab, n_grp, a_blocks, neighbors, prolong, agg_ids, coarse_prolong, pairing):
    rows, slots, width, _ = a_blocks.shape
    aggs = coarse_prolong.shape[0]
    half = aggs // 2
    sizes = (n_slab, n_grp, rows, slots, width, aggs)
    a_chunks = 7
    dma = pltpu.SemaphoreType.DMA
    scratch = [
        pltpu.VMEM((rows, slots, width, width), BF16),
        pltpu.VMEM((rows, width, slots * width), BF16),
        pltpu.VMEM((3 * rows, width, width), BF16),
        pltpu.VMEM((rows, width // 2, 2 * width), BF16),
        pltpu.VMEM((2, rows, width // 2, 2 * width), BF16),
        pltpu.VMEM((rows, width, width), BF16),
        pltpu.VMEM((aggs, width, width), BF16),
        pltpu.VMEM((aggs, width, width), BF16),
        pltpu.VMEM((rows + 1, width, width), F32),
        pltpu.VMEM((REACH, aggs, width // 2, 2 * width), BF16),
        pltpu.VMEM((2 * REACH + 1, aggs, width // 2, 2 * width), BF16),
        pltpu.VMEM((aggs, width // 2, 2 * width), F32),
        pltpu.VMEM((aggs, width, width), F32),
        pltpu.VMEM((half, width, width), F32),
        pltpu.VMEM((half, width // 2, 2 * width), BF16),
        pltpu.VMEM((half, width // 2, 2 * width), BF16),
        pltpu.VMEM((8, 128), jnp.int32),
        pltpu.SMEM((8, 128), jnp.int32),
        dma((a_chunks,)),
        dma((2,)),
        dma,
        dma((2,)),
        dma((2, CHUNKS)),
        dma((2, CHUNKS)),
        dma((REACH,)),
        dma((2 * REACH + 1,)),
        dma,
        dma,
    ]
    smem = pl.BlockSpec(memory_space=pltpu.SMEM)
    vmem = pl.BlockSpec(memory_space=pltpu.VMEM)
    hbm = pl.BlockSpec(memory_space=pl.ANY)
    return pl.pallas_call(
        functools.partial(kernel, sizes),
        out_shape=(
            jax.ShapeDtypeStruct((aggs, width, width), F32),
            jax.ShapeDtypeStruct((half, width, width), F32),
        ),
        in_specs=[smem, vmem, smem, hbm, hbm, hbm],
        out_specs=(hbm, hbm),
        scratch_shapes=scratch,
        compiler_params=pltpu.CompilerParams(
            collective_id=0, has_side_effects=True, vmem_limit_bytes=56 * 2**20
        ),
    )(neighbors, agg_ids.reshape(1, rows), pairing, a_blocks, prolong, coarse_prolong)


def solution(mesh):
    placed = (
        P(("slab", "grp"), None, None, None),
        P(("slab", "grp"), None),
        P(("slab", "grp"), None, None),
        P(("slab", "grp")),
        P(("slab", "grp"), None, None),
        P(("slab", "grp"), None),
    )
    return jax.shard_map(
        functools.partial(on_device, mesh.shape["slab"], mesh.shape["grp"]),
        mesh=mesh,
        in_specs=placed,
        out_specs=(P(("slab", "grp"), None, None), P(("slab", "grp"), None, None)),
        check_vma=False,
    )
```

time: 196 us -> 47.9 us (0.24)
  the two profiles are of different devices: /device:TPU:98 before, /device:TPU:40 now
where the time goes in v1:
time: 47.9 us; the launch traced here: 47.5 us
  Pallas kernels  42.1 us (88%)
  local copies, waits for them, and re-layouts  4.84 us (10%)
  between operations  0.64 us (1%)
    pallas_call x1, Pallas kernels, on_device(): pl.pallas_call(functools.partial(kernel, sizes), out_shape=(jax.ShapeDtyp...  42.1 us
    unnamed x3, local copies, waits for them, and re-layouts  4.84 us

profile of v1, /device:TPU:40, one launch (start us, length us, event | category | flops | bytes accessed | tf_op | source)
XLA Modules:
  0.0 47.5 jit_solution(11452660561028972325)
XLA Ops:
  0.6 1.4 %copy.8.nbr = s32[56,8]{1,0:T(8,128)} copy(s32[56,8]{0,1:T(8,128)} %param.7) | data formatting | bytes 3584 | tf_op args[1]
  2.0 42.1 %shard_map.77 = (f32[14,64,64]{2,1,0:T(8,128)}, f32[7,64,64]{2,1,0:T(8,128)}) custom-call(s32[56,8]{1,0:T(8,128)} %copy.8.nbr, s32[1,56]{1,0:T(1,128)} %bitcast.1, s32[1,7]{1,0:T(1,128)} %pair.1, bf16[56,8,64,64]{3,2,1,0:T(8,128)(2,1)} %a_hbm.1, bf16[56,64,64]{2,1,0:T(8,128)(2,1)} %p_hbm.1, bf16[14,64,64]{2,1,0:T(8,128)(2,1)} %m_hbm.1), custom_call_target="tpu_custom_call" | custom-call | tf_op jit(solution)/shard_map/pallas_call | solution.py:364
  44.1 1.8 %copy.11 = f32[14,64,64]{2,1,0:T(8,128)} copy(f32[14,64,64]{2,1,0:T(8,128)} %get-tuple-element.4) | data formatting | bytes 458752
  45.9 1.6 %copy.12 = f32[7,64,64]{2,1,0:T(8,128)} copy(f32[7,64,64]{2,1,0:T(8,128)} %get-tuple-element.5) | data formatting | bytes 229376

commit v2 on v1

--- a/solution.py
+++ b/solution.py
@@ -40,10 +40,10 @@
 
 def kernel(
     sizes,
-    nbr, agg, pair, a_hbm, p_hbm, m_hbm,
-    one_hbm, two_hbm,
-    a_buf, a_cat, ext, p_fold, halo, p_t, m_buf, m_t, run, send, recv, acc, one_buf, two_buf, tx, rx, tab_v, tab,
-    a_sem, in_sem, tab_sem, out_sem, halo_send, halo_recv, part_send, part_recv, pair_send, pair_recv,
+    nbr_hbm, agg_hbm, pair_hbm, a_hbm, p_hbm, m_hbm,
+    acc, two,
+    nbr, agg, pair, a_buf, a_cat, ext, p_fold, halo, p_t, m_buf, m_t, w_buf, run, send, recv, one_buf, tx, rx, tab_v, tab,
+    a_sem, in_sem, tab_sem, halo_send, halo_recv, part_send, part_recv, pair_send, pair_recv,
 ):
     n_slab, n_grp, rows, slots, width, aggs = sizes
     half = aggs // 2
@@ -62,6 +62,13 @@
     p_copy = pltpu.make_async_copy(p_hbm, ext.at[pl.ds(rows, rows)], in_sem.at[0])
     p_copy.start()
     m_copy = pltpu.make_async_copy(m_hbm, m_buf, in_sem.at[1])
+    small = [
+        pltpu.make_async_copy(agg_hbm, agg, in_sem.at[2]),
+        pltpu.make_async_copy(pair_hbm, pair, in_sem.at[3]),
+        pltpu.make_async_copy(nbr_hbm, nbr, in_sem.at[4]),
+    ]
+    for copy in small:
+        copy.start()
     a_chunks = a_sem.shape[0]
     a_rows = rows // a_chunks
     a_copies = [
@@ -108,7 +115,7 @@
             p_fold[chunk * per + r] = fold(ext[rows + chunk * per + r])
             return 0
 
-        lax.fori_loop(0, per, fold_row, 0, unroll=2)
+        lax.fori_loop(0, per, fold_row, 0, unroll=per)
         if chunk == 0:
             pl.semaphore_wait(barrier, WINDOW)
 
@@ -134,6 +141,8 @@
     lane = lax.broadcasted_iota(jnp.int32, (tall, 128), 1)
     lane_row = lax.broadcasted_iota(jnp.int32, (1, 128), 1)
     tab_v[...] = jnp.zeros_like(tab_v)
+    for copy in small:
+        copy.wait()
     tab_v[0:1, 0:rows] = agg[...]
     ids = tab_v[0:1, :]
     owner_row = lax.div(ids, jnp.int32(n_grp * aggs))
@@ -185,14 +194,14 @@
             p_t[row] = ext[rows + row].T
             return 0
 
-        lax.fori_loop(0, a_rows, lay, 0, unroll=2)
+        lax.fori_loop(0, a_rows, lay, 0, unroll=a_rows)
     m_copy.wait()
 
     def turn(k, _):
         m_t[k] = m_buf[k].T
         return 0
 
-    lax.fori_loop(0, aggs, turn, 0, unroll=2)
+    lax.fori_loop(0, aggs, turn, 0, unroll=half)
     tab_copy.wait()
 
     for side, there in ((0, has_previous), (1, has_next)):
@@ -218,7 +227,7 @@
                     ext[base + r] = unfold(halo[side, chunk * per + r])
                     return 0
 
-                lax.fori_loop(0, per, open_row, 0, unroll=2)
+                lax.fori_loop(0, per, open_row, 0, unroll=per)
 
     def part_copy(q):
         owner = first + bucket_of[q]
@@ -232,17 +241,26 @@
             device_id_type=MESH,
         )
 
-    def row_step(k, _):
-        r = jnp.clip(tab[0, k], 0, rows - 1)
-        picked = jnp.concatenate([ext[nbr[r, n]] for n in range(slots)], axis=0)
-        partial_w = jnp.dot(a_cat[r], picked, preferred_element_type=F32).astype(BF16)
-        part = jnp.dot(p_t[r], partial_w, preferred_element_type=F32)
+    def row_at(k):
+        return jnp.clip(tab[0, k], 0, rows - 1)
+
+    def weigh(k, _):
+        r = row_at(k)
+        picked = jnp.concatenate(
+            [ext[jnp.clip(nbr[n, r], 0, 3 * rows - 1)] for n in range(slots)], axis=0
+        )
+        w_buf[k] = jnp.dot(a_cat[r], picked, preferred_element_type=F32).astype(BF16)
+        return 0
+
+    def project(k, _):
+        part = jnp.dot(p_t[row_at(k)], w_buf[k], preferred_element_type=F32)
         run[k] = part + run[jnp.clip(tab[1, k], 0, rows)]
         return 0
 
     for q in range(WINDOW):
         begin, end = q * capacity, min((q + 1) * capacity, rows)
-        lax.fori_loop(begin, end, row_step, 0, unroll=4)
+        lax.fori_loop(begin, end, weigh, 0, unroll=end - begin)
+        lax.fori_loop(begin, end, project, 0, unroll=end - begin)
 
         def gather(k, _, q=q):
             block = fold(run[jnp.clip(tab[2, q * aggs + k], 0, rows)])
@@ -252,7 +270,7 @@
                 acc[k] = block
             return 0
 
-        lax.fori_loop(0, aggs, gather, 0, unroll=2)
+        lax.fori_loop(0, aggs, gather, 0, unroll=aggs)
         if q < REACH:
             part_copy(q).start()
 
@@ -276,9 +294,7 @@
         one_buf[k] = unfold(acc[k])
         return 0
 
-    lax.fori_loop(0, aggs, open_sum, 0, unroll=2)
-    one_copy = pltpu.make_async_copy(one_buf, one_hbm, out_sem.at[0])
-    one_copy.start()
+    lax.fori_loop(0, aggs, open_sum, 0, unroll=aggs)
 
     def away(t, _):
         k = jnp.where(parity == 0, half + t, jnp.clip(tab[3, t], 0, aggs - 1))
@@ -293,8 +309,8 @@
     pair_copy.start()
 
     def home(t, _):
-        k = jnp.where(parity == 0, t, pair[0, t])
-        two_buf[t] = galerkin(one_buf[k], m_t[k], m_buf[k])
+        k = jnp.where(parity == 0, t, jnp.clip(pair[0, t], 0, aggs - 1))
+        two[t] = fold(galerkin(one_buf[k], m_t[k], m_buf[k]))
         return 0
 
     lax.fori_loop(0, half, home, 0, unroll=half)
@@ -302,9 +318,7 @@
     for t in range(half):
         before = sum((pair[0, i] < pair[0, t]).astype(jnp.int32) for i in range(half))
         at_rx = jnp.where(parity == 0, before, t)
-        two_buf[t] += unfold(rx[at_rx].astype(F32))
-    two_copy = pltpu.make_async_copy(two_buf, two_hbm, out_sem.at[1])
-    two_copy.start()
+        two[t] += rx[at_rx].astype(F32)
 
     pair_copy.wait_send()
     for q in range(REACH):
@@ -317,6 +331,17 @@
         @pl.when(has_previous)
         def _():
             halo_copy(1, chunk).wait_send()
+
+
+def spread(acc, two_folded, one_hbm, two_hbm, one_buf, two_buf, sem):
+    for k in range(acc.shape[0]):
+        one_buf[k] = unfold(acc[k])
+    one_copy = pltpu.make_async_copy(one_buf, one_hbm, sem.at[0])
+    one_copy.start()
+    for k in range(two_folded.shape[0]):
+        two_buf[k] = unfold(two_folded[k])
+    two_copy = pltpu.make_async_copy(two_buf, two_hbm, sem.at[1])
+    two_copy.start()
     one_copy.wait()
     two_copy.wait()
 
@@ -329,6 +354,9 @@
     a_chunks = 7
     dma = pltpu.SemaphoreType.DMA
     scratch = [
+        pltpu.SMEM((slots, rows), jnp.int32),
+        pltpu.VMEM((1, rows), jnp.int32),
+        pltpu.SMEM((1, half), jnp.int32),
         pltpu.VMEM((rows, slots, width, width), BF16),
         pltpu.VMEM((rows, width, slots * width), BF16),
         pltpu.VMEM((3 * rows, width, width), BF16),
@@ -337,20 +365,18 @@
         pltpu.VMEM((rows, width, width), BF16),
         pltpu.VMEM((aggs, width, width), BF16),
         pltpu.VMEM((aggs, width, width), BF16),
+        pltpu.VMEM((rows, width, width), BF16),
         pltpu.VMEM((rows + 1, width, width), F32),
         pltpu.VMEM((REACH, aggs, width // 2, 2 * width), BF16),
         pltpu.VMEM((2 * REACH + 1, aggs, width // 2, 2 * width), BF16),
-        pltpu.VMEM((aggs, width // 2, 2 * width), F32),
         pltpu.VMEM((aggs, width, width), F32),
-        pltpu.VMEM((half, width, width), F32),
         pltpu.VMEM((half, width // 2, 2 * width), BF16),
         pltpu.VMEM((half, width // 2, 2 * width), BF16),
         pltpu.VMEM((8, 128), jnp.int32),
         pltpu.SMEM((8, 128), jnp.int32),
         dma((a_chunks,)),
-        dma((2,)),
+        dma((5,)),
         dma,
-        dma((2,)),
         dma((2, CHUNKS)),
         dma((2, CHUNKS)),
         dma((REACH,)),
@@ -358,22 +384,36 @@
         dma,
         dma,
     ]
-    smem = pl.BlockSpec(memory_space=pltpu.SMEM)
     vmem = pl.BlockSpec(memory_space=pltpu.VMEM)
-    hbm = pl.BlockSpec(memory_space=pl.ANY)
+    hbm = pl.BlockSpec(memory_space=pltpu.HBM)
+    folded = pl.pallas_call(
+        functools.partial(kernel, sizes),
+        out_shape=(
+            jax.ShapeDtypeStruct((aggs, width // 2, 2 * width), F32),
+            jax.ShapeDtypeStruct((half, width // 2, 2 * width), F32),
+        ),
+        in_specs=[hbm] * 6,
+        out_specs=(vmem, vmem),
+        scratch_shapes=scratch,
+        compiler_params=pltpu.CompilerParams(
+            collective_id=0, has_side_effects=True, vmem_limit_bytes=30 * 2**20
+        ),
+    )(*(pltpu.with_memory_space_constraint(x, pltpu.HBM) for x in (neighbors.T, agg_ids.reshape(1, rows), pairing, a_blocks, prolong, coarse_prolong)))
     return pl.pallas_call(
-        functools.partial(kernel, sizes),
+        spread,
         out_shape=(
             jax.ShapeDtypeStruct((aggs, width, width), F32),
             jax.ShapeDtypeStruct((half, width, width), F32),
         ),
-        in_specs=[smem, vmem, smem, hbm, hbm, hbm],
+        in_specs=[vmem, vmem],
         out_specs=(hbm, hbm),
-        scratch_shapes=scratch,
-        compiler_params=pltpu.CompilerParams(
-            collective_id=0, has_side_effects=True, vmem_limit_bytes=56 * 2**20
-        ),
-    )(neighbors, agg_ids.reshape(1, rows), pairing, a_blocks, prolong, coarse_prolong)
+        scratch_shapes=[
+            pltpu.VMEM((aggs, width, width), F32),
+            pltpu.VMEM((half, width, width), F32),
+            dma((2,)),
+        ],
+        compiler_params=pltpu.CompilerParams(vmem_limit_bytes=4 * 2**20),
+    )(*folded)
 
 
 def solution(mesh):

time: 47.9 us -> 33.4 us (0.70)
  the two profiles are of different devices: /device:TPU:40 before, /device:TPU:32 now
where the time goes in v2:
time: 33.4 us; the launch traced here: 33 us
  Pallas kernels  32.4 us (97%)
  between operations  0.64 us (2%)
    pallas_call x1, Pallas kernels, on_device(): pl.pallas_call(functools.partial(kernel, sizes), out_shape=(jax.ShapeDtyp...  31.4 us
    pallas_call x1, Pallas kernels, on_device(): pl.pallas_call(spread, out_shape=(jax.ShapeDtypeStruct((aggs, width, widt...  0.98 us

profile of v2, /device:TPU:32, one launch (start us, length us, event | category | flops | bytes accessed | tf_op | source)
XLA Modules:
  0.0 33.0 jit_solution(10343488485290649448)
XLA Ops:
  0.6 31.4 %shard_map.77 = (f32[14,32,128]{2,1,0:T(8,128)S(1)}, f32[7,32,128]{2,1,0:T(8,128)S(1)}) custom-call(s32[8,56]{1,0:T(8,128)} %bitcast.2, s32[1,56]{1,0:T(1,128)} %bitcast.3, s32[1,7]{1,0:T(1,128)} %pair_hbm.1, bf16[56,8,64,64]{3,2,1,0:T(8,128)(2,1)} %a_hbm.1, bf16[56,64,64]{2,1,0:T(8,128)(2,1)} %p_hbm.1, bf16[14,64,64]{2,1,0:T(8,128)(2,1)} %m_hbm.1), custom_call_target="tpu_custom_call" | custom-call | tf_op jit(solution)/shard_map/pallas_call | solution.py:389
  32.0 1.0 %shard_map.78 = (f32[14,64,64]{2,1,0:T(8,128)}, f32[7,64,64]{2,1,0:T(8,128)}) custom-call(f32[14,32,128]{2,1,0:T(8,128)S(1)} %get-tuple-element.4.acc, f32[7,32,128]{2,1,0:T(8,128)S(1)} %get-tuple-element.5.two_folded), custom_call_target="tpu_custom_call" | custom-call | tf_op jit(solution)/shard_map/pallas_call | solution.py:402

commit v3 on v2

--- a/solution.py
+++ b/solution.py
@@ -10,6 +10,8 @@
 MESH = pl.DeviceIdType.MESH
 WINDOW = 5
 REACH = WINDOW - 1
+HANDED, SHARED = 1, 2
+OFFSETS = (-1, 1, -2, 2, -4, 4)
 CHUNKS = 4
 F32 = jnp.float32
 BF16 = jnp.bfloat16
@@ -42,8 +44,8 @@
     sizes,
     nbr_hbm, agg_hbm, pair_hbm, a_hbm, p_hbm, m_hbm,
     acc, two,
-    nbr, agg, pair, a_buf, a_cat, ext, p_fold, halo, p_t, m_buf, m_t, w_buf, run, send, recv, one_buf, tx, rx, tab_v, tab,
-    a_sem, in_sem, tab_sem, halo_send, halo_recv, part_send, part_recv, pair_send, pair_recv,
+    nbr, agg, pair, a_buf, a_cat, ext, p_fold, halo, p_t, m_buf, m_t, w_buf, run, send, recv, hand, handed, one_buf, tx, rx, tab_v, tab,
+    a_sem, p_sem, in_sem, tab_sem, halo_send, halo_recv, part_send, part_recv, hand_recv, pair_send, pair_recv,
 ):
     n_slab, n_grp, rows, slots, width, aggs = sizes
     half = aggs // 2
@@ -51,16 +53,33 @@
     slab = lax.axis_index("slab")
     grp = lax.axis_index("grp")
 
-    def window(s):
-        return jnp.clip(s - WINDOW // 2, 0, n_slab - WINDOW)
-
-    first = window(slab)
-    chip_mate = slab + 1 - 2 * (slab % 2)
+    def owners(s):
+        odd = s % 2
+        side = 1 - 2 * odd
+        low, high = s < 2, s >= n_slab - 2
+        end = low | high
+        direct = jnp.where(low, 2, jnp.where(high, n_slab - 3, s - 2 * side))
+        far = jnp.where(low, 4, n_slab - 5)
+        near = jnp.where(low, 3, n_slab - 4)
+        outer = jnp.where(low, odd == 0, odd == 1)
+        handed = jnp.where(end, jnp.where(outer, near, far), s + 2 * side)
+        shared = jnp.where(end, jnp.where(outer, far, near), s - side)
+        return direct, handed, shared, s + side, s
+
+    owner_of = owners(slab)
+    chip_mate = owner_of[3]
     grp_mate = grp + 1 - 2 * (grp % 2)
     parity = grp % 2
 
-    p_copy = pltpu.make_async_copy(p_hbm, ext.at[pl.ds(rows, rows)], in_sem.at[0])
-    p_copy.start()
+    per = rows // CHUNKS
+    p_copies = [
+        pltpu.make_async_copy(
+            p_hbm.at[pl.ds(i * per, per)], ext.at[pl.ds(rows + i * per, per)], p_sem.at[i]
+        )
+        for i in range(CHUNKS)
+    ]
+    for copy in p_copies:
+        copy.start()
     m_copy = pltpu.make_async_copy(m_hbm, m_buf, in_sem.at[1])
     small = [
         pltpu.make_async_copy(agg_hbm, agg, in_sem.at[2]),
@@ -83,18 +102,15 @@
 
     def sends_here(offset):
         source = slab + offset
-        low = window(source)
-        return (source >= 0) & (source < n_slab) & (low <= slab) & (slab < low + WINDOW)
-
-    for offset in range(-REACH, REACH + 1):
-        if offset != 0:
-            @pl.when(sends_here(offset))
-            def _():
-                pl.semaphore_signal(barrier, inc=1, device_id=(slab + offset, grp), device_id_type=MESH)
+        direct, _, shared, mate, _ = owners(source)
+        return (source >= 0) & (source < n_slab) & ((direct == slab) | (shared == slab) | (mate == slab))
+
+    senders = {offset: sends_here(offset) for offset in OFFSETS}
+    for offset in OFFSETS:
+        @pl.when(senders[offset])
+        def _():
+            pl.semaphore_signal(barrier, inc=1, device_id=(slab + offset, grp), device_id_type=MESH)
     pl.semaphore_signal(barrier, inc=1, device_id=(slab, grp_mate), device_id_type=MESH)
-
-    p_copy.wait()
-    per = rows // CHUNKS
 
     def halo_copy(side, chunk):
         span = pl.ds(chunk * per, per)
@@ -111,13 +127,15 @@
     has_next = slab < n_slab - 1
     has_previous = slab > 0
     for chunk in range(CHUNKS):
+        p_copies[chunk].wait()
+
         def fold_row(r, _, chunk=chunk):
             p_fold[chunk * per + r] = fold(ext[rows + chunk * per + r])
             return 0
 
         lax.fori_loop(0, per, fold_row, 0, unroll=per)
         if chunk == 0:
-            pl.semaphore_wait(barrier, WINDOW)
+            pl.semaphore_wait(barrier, 4)
 
         @pl.when(has_next)
         def _():
@@ -127,15 +145,6 @@
         def _():
             halo_copy(1, chunk).start()
 
-    tag = []
-    for j in range(WINDOW):
-        owner = first + j
-        kind = jnp.where(owner == slab, 2, jnp.where(owner == chip_mate, 1, 0))
-        tag.append(kind * WINDOW + j)
-    place = [sum((tag[i] < tag[j]).astype(jnp.int32) for i in range(WINDOW)) for j in range(WINDOW)]
-    bucket_of = [
-        sum(jnp.where(place[j] == q, j, 0) for j in range(WINDOW)) for q in range(WINDOW)
-    ]
     tall = 64
     sub = lax.broadcasted_iota(jnp.int32, (tall, 128), 0)
     lane = lax.broadcasted_iota(jnp.int32, (tall, 128), 1)
@@ -147,10 +156,9 @@
     ids = tab_v[0:1, :]
     owner_row = lax.div(ids, jnp.int32(n_grp * aggs))
     inside = lax.rem(ids, jnp.int32(aggs))
-    bucket = owner_row - first
-    at = jnp.zeros_like(bucket)
-    for j in range(WINDOW):
-        at = at + jnp.where(bucket == j, place[j], 0)
+    at = jnp.zeros_like(owner_row)
+    for q in range(WINDOW):
+        at = at + jnp.where(owner_row == owner_of[q], q, 0)
     far = 1000
     key_row = jnp.where(lane_row < rows, at * aggs + inside, far).astype(F32)
     keys = jnp.broadcast_to(key_row, (tall, 128))
@@ -230,14 +238,18 @@
                 lax.fori_loop(0, per, open_row, 0, unroll=per)
 
     def part_copy(q):
-        owner = first + bucket_of[q]
+        owner = owner_of[q]
         at_owner = slab - owner + REACH
+        if q == HANDED:
+            source, target, arrived = hand, handed, hand_recv
+        else:
+            source, target, arrived = send.at[q], recv.at[at_owner], part_recv.at[at_owner]
         return pltpu.make_async_remote_copy(
-            src_ref=send.at[q],
-            dst_ref=recv.at[at_owner],
+            src_ref=source,
+            dst_ref=target,
             send_sem=part_send.at[q],
-            recv_sem=part_recv.at[at_owner],
-            device_id=(owner, grp),
+            recv_sem=arrived,
+            device_id=(chip_mate if q == HANDED else owner, grp),
             device_id_type=MESH,
         )
 
@@ -264,21 +276,27 @@
 
         def gather(k, _, q=q):
             block = fold(run[jnp.clip(tab[2, q * aggs + k], 0, rows)])
-            if q < REACH:
+            if q == HANDED:
+                hand[k] = block
+            elif q == SHARED:
+                send[q, k] = (block + handed[k]).astype(BF16)
+            elif q < REACH:
                 send[q, k] = block.astype(BF16)
             else:
                 acc[k] = block
             return 0
 
+        if q == SHARED:
+            part_copy(HANDED).wait_recv()
+
         lax.fori_loop(0, aggs, gather, 0, unroll=aggs)
         if q < REACH:
             part_copy(q).start()
 
-    offsets = sorted((d for d in range(-REACH, REACH + 1) if d != 0), key=abs)
-    for offset in offsets:
+    for offset in OFFSETS:
         at_here = offset + REACH
 
-        @pl.when(sends_here(offset))
+        @pl.when(senders[offset])
         def _():
             pltpu.make_async_remote_copy(
                 src_ref=recv.at[at_here],
@@ -369,18 +387,22 @@
         pltpu.VMEM((rows + 1, width, width), F32),
         pltpu.VMEM((REACH, aggs, width // 2, 2 * width), BF16),
         pltpu.VMEM((2 * REACH + 1, aggs, width // 2, 2 * width), BF16),
+        pltpu.VMEM((aggs, width // 2, 2 * width), F32),
+        pltpu.VMEM((aggs, width // 2, 2 * width), F32),
         pltpu.VMEM((aggs, width, width), F32),
         pltpu.VMEM((half, width // 2, 2 * width), BF16),
         pltpu.VMEM((half, width // 2, 2 * width), BF16),
         pltpu.VMEM((8, 128), jnp.int32),
         pltpu.SMEM((8, 128), jnp.int32),
         dma((a_chunks,)),
+        dma((CHUNKS,)),
         dma((5,)),
         dma,
         dma((2, CHUNKS)),
         dma((2, CHUNKS)),
         dma((REACH,)),
         dma((2 * REACH + 1,)),
+        dma,
         dma,
         dma,
     ]

time: 33.4 us -> 32.5 us (0.973)
  Pallas kernels: 32.4 us -> 31.7 us
    pallas_call x1, Pallas kernels: 31.4 us -> 30.7 us  [on_device(): pl.pallas_call(functools.partial(kernel, sizes), out_shape=(jax.ShapeDtyp...]
where the time goes in v3:
time: 32.5 us; the launch traced here: 32.4 us
  Pallas kernels  31.7 us (98%)
  between operations  0.64 us (2%)
    pallas_call x1, Pallas kernels, on_device(): pl.pallas_call(functools.partial(kernel, sizes), out_shape=(jax.ShapeDtyp...  30.7 us
    pallas_call x1, Pallas kernels, on_device(): pl.pallas_call(spread, out_shape=(jax.ShapeDtypeStruct((aggs, width, widt...  0.98 us

profile of v3, /device:TPU:32, one launch (start us, length us, event | category | flops | bytes accessed | tf_op | source)
XLA Modules:
  0.0 32.4 jit_solution(12428995437032034749)
XLA Ops:
  0.6 30.7 %shard_map.77 = (f32[14,32,128]{2,1,0:T(8,128)S(1)}, f32[7,32,128]{2,1,0:T(8,128)S(1)}) custom-call(s32[8,56]{1,0:T(8,128)} %bitcast.2, s32[1,56]{1,0:T(1,128)} %bitcast.3, s32[1,7]{1,0:T(1,128)} %pair_hbm.1, bf16[56,8,64,64]{3,2,1,0:T(8,128)(2,1)} %a_hbm.1, bf16[56,64,64]{2,1,0:T(8,128)(2,1)} %p_hbm.1, bf16[14,64,64]{2,1,0:T(8,128)(2,1)} %m_hbm.1), custom_call_target="tpu_custom_call" | custom-call | tf_op jit(solution)/shard_map/pallas_call | solution.py:411
  31.4 1.0 %shard_map.78 = (f32[14,64,64]{2,1,0:T(8,128)}, f32[7,64,64]{2,1,0:T(8,128)}) custom-call(f32[14,32,128]{2,1,0:T(8,128)S(1)} %get-tuple-element.4.acc, f32[7,32,128]{2,1,0:T(8,128)S(1)} %get-tuple-element.5.two_folded), custom_call_target="tpu_custom_call" | custom-call | tf_op jit(solution)/shard_map/pallas_call | solution.py:424

commit v4 on v3

--- a/solution.py
+++ b/solution.py
@@ -11,7 +11,7 @@
 WINDOW = 5
 REACH = WINDOW - 1
 HANDED, SHARED = 1, 2
-OFFSETS = (-1, 1, -2, 2, -4, 4)
+OFFSETS = (4, 2, 1, -1, -2, -4)
 CHUNKS = 4
 F32 = jnp.float32
 BF16 = jnp.bfloat16
@@ -70,6 +70,26 @@
     chip_mate = owner_of[3]
     grp_mate = grp + 1 - 2 * (grp % 2)
     parity = grp % 2
+
+    barrier = pltpu.get_barrier_semaphore()
+
+    def sends_here(offset):
+        source = slab + offset
+        direct, _, shared, mate, _ = owners(source)
+        return (source >= 0) & (source < n_slab) & ((direct == slab) | (shared == slab) | (mate == slab))
+
+    def greets(offset):
+        source = slab + offset
+        direct, _, shared, mate, _ = owners(source)
+        end = (source < 2) | (source >= n_slab - 2)
+        return (source >= 0) & (source < n_slab) & ((end & (direct == slab)) | (shared == slab) | (mate == slab))
+
+    senders = {offset: sends_here(offset) for offset in OFFSETS}
+    for offset in OFFSETS:
+        @pl.when(greets(offset))
+        def _():
+            pl.semaphore_signal(barrier, inc=1, device_id=(slab + offset, grp), device_id_type=MESH)
+    pl.semaphore_signal(barrier, inc=1, device_id=(slab, grp_mate), device_id_type=MESH)
 
     per = rows // CHUNKS
     p_copies = [
@@ -98,20 +118,6 @@
         copy.start()
     m_copy.start()
 
-    barrier = pltpu.get_barrier_semaphore()
-
-    def sends_here(offset):
-        source = slab + offset
-        direct, _, shared, mate, _ = owners(source)
-        return (source >= 0) & (source < n_slab) & ((direct == slab) | (shared == slab) | (mate == slab))
-
-    senders = {offset: sends_here(offset) for offset in OFFSETS}
-    for offset in OFFSETS:
-        @pl.when(senders[offset])
-        def _():
-            pl.semaphore_signal(barrier, inc=1, device_id=(slab + offset, grp), device_id_type=MESH)
-    pl.semaphore_signal(barrier, inc=1, device_id=(slab, grp_mate), device_id_type=MESH)
-
     def halo_copy(side, chunk):
         span = pl.ds(chunk * per, per)
         target = slab + 1 - 2 * side
@@ -135,7 +141,7 @@
 
         lax.fori_loop(0, per, fold_row, 0, unroll=per)
         if chunk == 0:
-            pl.semaphore_wait(barrier, 4)
+            pl.semaphore_wait(barrier, jnp.where((slab < 2) | (slab >= n_slab - 2), 4, 3))
 
         @pl.when(has_next)
         def _():
@@ -237,21 +243,29 @@
 
                 lax.fori_loop(0, per, open_row, 0, unroll=per)
 
-    def part_copy(q):
+    def part_copy(q, piece=0):
         owner = owner_of[q]
         at_owner = slab - owner + REACH
         if q == HANDED:
             source, target, arrived = hand, handed, hand_recv
         else:
-            source, target, arrived = send.at[q], recv.at[at_owner], part_recv.at[at_owner]
+            span = pl.ds(piece * half, half)
+            source, target, arrived = send.at[q, span], recv.at[at_owner, span], part_recv.at[at_owner, piece]
         return pltpu.make_async_remote_copy(
             src_ref=source,
             dst_ref=target,
-            send_sem=part_send.at[q],
+            send_sem=part_send.at[q, piece],
             recv_sem=arrived,
             device_id=(chip_mate if q == HANDED else owner, grp),
             device_id_type=MESH,
         )
+
+    leaves = {
+        0: ((0, 0), (0, 1)),
+        HANDED: ((HANDED, 0),),
+        SHARED: ((SHARED, 0), (SHARED, 1)),
+        3: ((3, 0), (3, 1)),
+    }
 
     def row_at(k):
         return jnp.clip(tab[0, k], 0, rows - 1)
@@ -290,23 +304,25 @@
             part_copy(HANDED).wait_recv()
 
         lax.fori_loop(0, aggs, gather, 0, unroll=aggs)
-        if q < REACH:
-            part_copy(q).start()
+        for which in leaves.get(q, ()):
+            part_copy(*which).start()
 
     for offset in OFFSETS:
         at_here = offset + REACH
 
         @pl.when(senders[offset])
         def _():
-            pltpu.make_async_remote_copy(
-                src_ref=recv.at[at_here],
-                dst_ref=recv.at[at_here],
-                send_sem=part_send.at[0],
-                recv_sem=part_recv.at[at_here],
-                device_id=(slab, grp),
-                device_id_type=MESH,
-            ).wait_recv()
-            acc[...] += recv[at_here].astype(F32)
+            for piece in range(2):
+                span = pl.ds(piece * half, half)
+                pltpu.make_async_remote_copy(
+                    src_ref=recv.at[at_here, span],
+                    dst_ref=recv.at[at_here, span],
+                    send_sem=part_send.at[0, piece],
+                    recv_sem=part_recv.at[at_here, piece],
+                    device_id=(slab, grp),
+                    device_id_type=MESH,
+                ).wait_recv()
+                acc[span] += recv[at_here, span].astype(F32)
 
     def open_sum(k, _):
         one_buf[k] = unfold(acc[k])
@@ -319,12 +335,19 @@
         tx[t] = fold(galerkin(one_buf[k], m_t[k], m_buf[k])).astype(BF16)
         return 0
 
-    lax.fori_loop(0, half, away, 0, unroll=half)
-    pair_copy = pltpu.make_async_remote_copy(
-        src_ref=tx, dst_ref=rx, send_sem=pair_send, recv_sem=pair_recv,
-        device_id=(slab, grp_mate), device_id_type=MESH,
-    )
-    pair_copy.start()
+    cut = (half + 1) // 2
+    pair_copies = []
+    for piece, (begin, end) in enumerate(((0, cut), (cut, half))):
+        lax.fori_loop(begin, end, away, 0, unroll=end - begin)
+        span = pl.ds(begin, end - begin)
+        pair_copies.append(
+            pltpu.make_async_remote_copy(
+                src_ref=tx.at[span], dst_ref=rx.at[span],
+                send_sem=pair_send.at[piece], recv_sem=pair_recv.at[piece],
+                device_id=(slab, grp_mate), device_id_type=MESH,
+            )
+        )
+        pair_copies[-1].start()
 
     def home(t, _):
         k = jnp.where(parity == 0, t, jnp.clip(pair[0, t], 0, aggs - 1))
@@ -332,15 +355,19 @@
         return 0
 
     lax.fori_loop(0, half, home, 0, unroll=half)
-    pair_copy.wait_recv()
+    at_rx = []
     for t in range(half):
         before = sum((pair[0, i] < pair[0, t]).astype(jnp.int32) for i in range(half))
-        at_rx = jnp.where(parity == 0, before, t)
-        two[t] += rx[at_rx].astype(F32)
-
-    pair_copy.wait_send()
-    for q in range(REACH):
-        part_copy(q).wait_send()
+        at_rx.append(jnp.where(parity == 0, jnp.clip(before, 0, half - 1), t))
+    for copy in pair_copies:
+        copy.wait_recv()
+    for t in range(half):
+        two[t] += rx[at_rx[t]].astype(F32)
+
+    for copy in pair_copies:
+        copy.wait_send()
+    for which in sum(leaves.values(), ()):
+        part_copy(*which).wait_send()
     for chunk in range(CHUNKS):
         @pl.when(has_next)
         def _():
@@ -400,11 +427,11 @@
         dma,
         dma((2, CHUNKS)),
         dma((2, CHUNKS)),
-        dma((REACH,)),
-        dma((2 * REACH + 1,)),
+        dma((REACH, 2)),
+        dma((2 * REACH + 1, 2)),
         dma,
-        dma,
-        dma,
+        dma((2,)),
+        dma((2,)),
     ]
     vmem = pl.BlockSpec(memory_space=pltpu.VMEM)
     hbm = pl.BlockSpec(memory_space=pltpu.HBM)

time: 32.5 us -> 31.9 us (0.982)
  Pallas kernels: 31.7 us -> 31.2 us
    pallas_call x1, Pallas kernels: 30.7 us -> 30.2 us  [on_device(): pl.pallas_call(functools.partial(kernel, sizes), out_shape=(jax.ShapeDtyp...]
where the time goes in v4:
time: 31.9 us; the launch traced here: 31.8 us
  Pallas kernels  31.2 us (98%)
  between operations  0.64 us (2%)
    pallas_call x1, Pallas kernels, on_device(): pl.pallas_call(functools.partial(kernel, sizes), out_shape=(jax.ShapeDtyp...  30.2 us
    pallas_call x1, Pallas kernels, on_device(): pl.pallas_call(spread, out_shape=(jax.ShapeDtypeStruct((aggs, width, widt...  0.98 us

profile of v4, /device:TPU:32, one launch (start us, length us, event | category | flops | bytes accessed | tf_op | source)
XLA Modules:
  0.0 31.8 jit_solution(5660881541682339979)
XLA Ops:
  0.6 30.2 %shard_map.77 = (f32[14,32,128]{2,1,0:T(8,128)S(1)}, f32[7,32,128]{2,1,0:T(8,128)S(1)}) custom-call(s32[8,56]{1,0:T(8,128)} %bitcast.2, s32[1,56]{1,0:T(1,128)} %bitcast.3, s32[1,7]{1,0:T(1,128)} %pair_hbm.1, bf16[56,8,64,64]{3,2,1,0:T(8,128)(2,1)} %a_hbm.1, bf16[56,64,64]{2,1,0:T(8,128)(2,1)} %p_hbm.1, bf16[14,64,64]{2,1,0:T(8,128)(2,1)} %m_hbm.1), custom_call_target="tpu_custom_call" | custom-call | tf_op jit(solution)/shard_map/pallas_call | solution.py:438
  30.8 1.0 %shard_map.78 = (f32[14,64,64]{2,1,0:T(8,128)}, f32[7,64,64]{2,1,0:T(8,128)}) custom-call(f32[14,32,128]{2,1,0:T(8,128)S(1)} %get-tuple-element.4.acc, f32[7,32,128]{2,1,0:T(8,128)S(1)} %get-tuple-element.5.two_folded), custom_call_target="tpu_custom_call" | custom-call | tf_op jit(solution)/shard_map/pallas_call | solution.py:451

commit v5 on v4

--- a/solution.py
+++ b/solution.py
@@ -12,7 +12,7 @@
 REACH = WINDOW - 1
 HANDED, SHARED = 1, 2
 OFFSETS = (4, 2, 1, -1, -2, -4)
-CHUNKS = 4
+CHUNKS = 8
 F32 = jnp.float32
 BF16 = jnp.bfloat16
 
@@ -273,7 +273,7 @@
     def weigh(k, _):
         r = row_at(k)
         picked = jnp.concatenate(
-            [ext[jnp.clip(nbr[n, r], 0, 3 * rows - 1)] for n in range(slots)], axis=0
+            [ext[nbr[n, r]] for n in range(slots)], axis=0
         )
         w_buf[k] = jnp.dot(a_cat[r], picked, preferred_element_type=F32).astype(BF16)
         return 0

time: 31.9 us -> 31.8 us (level)
  no operation moved by 1% of the time
where the time goes in v5:
time: 31.8 us; the launch traced here: 31.7 us
  Pallas kernels  31 us (97%)
  between operations  0.64 us (2%)
    pallas_call x1, Pallas kernels, on_device(): pl.pallas_call(functools.partial(kernel, sizes), out_shape=(jax.ShapeDtyp...  30 us
    pallas_call x1, Pallas kernels, on_device(): pl.pallas_call(spread, out_shape=(jax.ShapeDtypeStruct((aggs, width, widt...  0.98 us

profile of v5, /device:TPU:32, one launch (start us, length us, event | category | flops | bytes accessed | tf_op | source)
XLA Modules:
  0.0 31.7 jit_solution(15243990691283016126)
XLA Ops:
  0.6 30.0 %shard_map.77 = (f32[14,32,128]{2,1,0:T(8,128)S(1)}, f32[7,32,128]{2,1,0:T(8,128)S(1)}) custom-call(s32[8,56]{1,0:T(8,128)} %bitcast.2, s32[1,56]{1,0:T(1,128)} %bitcast.3, s32[1,7]{1,0:T(1,128)} %pair_hbm.1, bf16[56,8,64,64]{3,2,1,0:T(8,128)(2,1)} %a_hbm.1, bf16[56,64,64]{2,1,0:T(8,128)(2,1)} %p_hbm.1, bf16[14,64,64]{2,1,0:T(8,128)(2,1)} %m_hbm.1), custom_call_target="tpu_custom_call" | custom-call | tf_op jit(solution)/shard_map/pallas_call | solution.py:438
  30.7 1.0 %shard_map.78 = (f32[14,64,64]{2,1,0:T(8,128)}, f32[7,64,64]{2,1,0:T(8,128)}) custom-call(f32[14,32,128]{2,1,0:T(8,128)S(1)} %get-tuple-element.4.acc, f32[7,32,128]{2,1,0:T(8,128)S(1)} %get-tuple-element.5.two_folded), custom_call_target="tpu_custom_call" | custom-call | tf_op jit(solution)/shard_map/pallas_call | solution.py:451

commit v6 on v5

--- a/solution.py
+++ b/solution.py
@@ -44,7 +44,7 @@
     sizes,
     nbr_hbm, agg_hbm, pair_hbm, a_hbm, p_hbm, m_hbm,
     acc, two,
-    nbr, agg, pair, a_buf, a_cat, ext, p_fold, halo, p_t, m_buf, m_t, w_buf, run, send, recv, hand, handed, one_buf, tx, rx, tab_v, tab,
+    nbr, agg, pair, a_buf, a_cat, ext, p_fold, halo, p_t, m_buf, m_t, run, send, recv, hand, handed, one_buf, tx, rx, tab_v, tab,
     a_sem, p_sem, in_sem, tab_sem, halo_send, halo_recv, part_send, part_recv, hand_recv, pair_send, pair_recv,
 ):
     n_slab, n_grp, rows, slots, width, aggs = sizes
@@ -270,23 +270,22 @@
     def row_at(k):
         return jnp.clip(tab[0, k], 0, rows - 1)
 
-    def weigh(k, _):
+    def weigh(k):
         r = row_at(k)
         picked = jnp.concatenate(
             [ext[nbr[n, r]] for n in range(slots)], axis=0
         )
-        w_buf[k] = jnp.dot(a_cat[r], picked, preferred_element_type=F32).astype(BF16)
-        return 0
-
-    def project(k, _):
-        part = jnp.dot(p_t[row_at(k)], w_buf[k], preferred_element_type=F32)
-        run[k] = part + run[jnp.clip(tab[1, k], 0, rows)]
-        return 0
+        return jnp.dot(a_cat[r], picked, preferred_element_type=F32).astype(BF16)
 
     for q in range(WINDOW):
         begin, end = q * capacity, min((q + 1) * capacity, rows)
-        lax.fori_loop(begin, end, weigh, 0, unroll=end - begin)
-        lax.fori_loop(begin, end, project, 0, unroll=end - begin)
+        weighed = [weigh(k) for k in range(begin, end)]
+        parts = [
+            jnp.dot(p_t[row_at(begin + i)], block, preferred_element_type=F32)
+            for i, block in enumerate(weighed)
+        ]
+        for i, part in enumerate(parts):
+            run[begin + i] = part + run[jnp.clip(tab[1, begin + i], 0, rows)]
 
         def gather(k, _, q=q):
             block = fold(run[jnp.clip(tab[2, q * aggs + k], 0, rows)])
@@ -410,7 +409,6 @@
         pltpu.VMEM((rows, width, width), BF16),
         pltpu.VMEM((aggs, width, width), BF16),
         pltpu.VMEM((aggs, width, width), BF16),
-        pltpu.VMEM((rows, width, width), BF16),
         pltpu.VMEM((rows + 1, width, width), F32),
         pltpu.VMEM((REACH, aggs, width // 2, 2 * width), BF16),
         pltpu.VMEM((2 * REACH + 1, aggs, width // 2, 2 * width), BF16),

time: 31.8 us -> 31.7 us (level)
  no operation moved by 1% of the time
where the time goes in v6:
time: 31.7 us; the launch traced here: 31.6 us
  Pallas kernels  30.9 us (97%)
  between operations  0.64 us (2%)
    pallas_call x1, Pallas kernels, on_device(): pl.pallas_call(functools.partial(kernel, sizes), out_shape=(jax.ShapeDtyp...  29.9 us
    pallas_call x1, Pallas kernels, on_device(): pl.pallas_call(spread, out_shape=(jax.ShapeDtypeStruct((aggs, width, widt...  0.98 us

profile of v6, /device:TPU:32, one launch (start us, length us, event | category | flops | bytes accessed | tf_op | source)
XLA Modules:
  0.0 31.6 jit_solution(844747989075332066)
XLA Ops:
  0.6 29.9 %shard_map.77 = (f32[14,32,128]{2,1,0:T(8,128)S(1)}, f32[7,32,128]{2,1,0:T(8,128)S(1)}) custom-call(s32[8,56]{1,0:T(8,128)} %bitcast.2, s32[1,56]{1,0:T(1,128)} %bitcast.3, s32[1,7]{1,0:T(1,128)} %pair_hbm.1, bf16[56,8,64,64]{3,2,1,0:T(8,128)(2,1)} %a_hbm.1, bf16[56,64,64]{2,1,0:T(8,128)(2,1)} %p_hbm.1, bf16[14,64,64]{2,1,0:T(8,128)(2,1)} %m_hbm.1), custom_call_target="tpu_custom_call" | custom-call | tf_op jit(solution)/shard_map/pallas_call | solution.py:436
  30.6 1.0 %shard_map.78 = (f32[14,64,64]{2,1,0:T(8,128)}, f32[7,64,64]{2,1,0:T(8,128)}) custom-call(f32[14,32,128]{2,1,0:T(8,128)S(1)} %get-tuple-element.4.acc, f32[7,32,128]{2,1,0:T(8,128)S(1)} %get-tuple-element.5.two_folded), custom_call_target="tpu_custom_call" | custom-call | tf_op jit(solution)/shard_map/pallas_call | solution.py:449
